TPU v7x, 32 devices: a whole 2x2x4 slice. The times are simulated.
32 devices in a mesh: groups: 2 (over y), lat: 4 (over z), chan: 2 (over x), lon: 2 (over core).
Axes of the slice: x: 2, y: 2, z: 4, core: 2. Of those that a mesh axis runs over, the one named last changes fastest.
Arguments:
- activations: bfloat16 [32, 192, 512], P(('groups', 'lat'), 'lon', 'chan'), parts along dimension 0, may hold values from -6 to 6
- cotangent: bfloat16 [32, 192, 512], P(('groups', 'lat'), 'lon', 'chan'), parts along dimension 0, may hold values from -6 to 6
- w_first: bfloat16 [3, 512, 512], P(None, None, 'chan'), may hold values from -0.15625 to 0.15625
- w_second: bfloat16 [3, 512, 512], P(None, None, 'chan'), may hold values from -0.15625 to 0.15625
- offsets: int32 [16, 6], replicated, may hold values from -1 to 1, as said below
- basis: int32 [16, 6], replicated, may hold values from 0 to 2
- live: int32 [16], replicated, may hold values from 2 to 6, as said below
- taps: float32 [16, 6, 3], replicated, may hold values from -3 to 3
Outputs:
- mixed_out: bfloat16 [32, 192, 512], P(('groups', 'lat'), 'lon', 'chan'), parts along dimension 0
- grad_input: float32 [32, 192, 512], P(('groups', 'lat'), 'lon', 'chan'), parts along dimension 0
- grad_first: float32 [6, 512, 512], P('groups', None, 'chan'), parts along dimension 0
- grad_second: float32 [6, 512, 512], P('groups', None, 'chan'), parts along dimension 0
There are 2 independent parts, one for each index of `groups`. A program takes and returns all parts, laid end to end along the dimension named above; an argument that names none is the same for every part. Nothing has to cross between parts.
Inputs may be any that keep to these rules, and one draw needn't show every extreme that they name: Row i + offsets[i, s] lies in the grid for every entry; row 8 has entries at both ends of the reach. `live`: every row i with min(i, 15 - i) < max(2, 1) uses all 6 entries; row 8 uses exactly 2.
All inputs are finite; a program needn't handle non-finite values.
Results may differ from a plain program's by a relative error of at most 0.012.
Values may be sent and summed in bfloat16 or wider, within the bound.
A program may use at most 64 MiB of HBM per device.

v0:
```python
import jax
import jax.numpy as jnp
from jax import lax
from jax.sharding import PartitionSpec as P

KB = 3
HALO = 1


def padded(cells, sides, width):
    for axis, dim in sides:
        count = lax.axis_size(axis)
        head = lax.slice_in_dim(cells, 0, width, axis=dim)
        tail = lax.slice_in_dim(cells, cells.shape[dim] - width, cells.shape[dim], axis=dim)
        cells = jnp.concatenate(
            [
                lax.ppermute(tail, axis, [(i, (i + 1) % count) for i in range(count)]),
                cells,
                lax.ppermute(head, axis, [((i + 1) % count, i) for i in range(count)]),
            ],
            axis=dim,
        )
    return cells


def coefficients(offsets, basis, live, taps):
    stencil = 2 * HALO + 1
    slot_count = offsets.shape[1]
    in_use = jnp.arange(slot_count)[None, :] < live[:, None]
    row_hit = (offsets[:, :, None] == (jnp.arange(stencil) - HALO)[None, None, :]) & in_use[
        :, :, None
    ]
    kind_hit = basis[:, :, None] == jnp.arange(KB)[None, None, :]
    chosen = row_hit[:, :, :, None] & kind_hit[:, :, None, :]
    return jnp.sum(
        jnp.where(chosen[..., None], taps[:, :, None, None, :], jnp.float32(0.0)), axis=1
    )


def spread(extended, coef_table):
    row_count = coef_table.shape[0]
    lon_count = extended.shape[1] - 2 * HALO
    stencil = 2 * HALO + 1
    summed = jnp.zeros((row_count, lon_count, KB, extended.shape[2]), jnp.float32)
    for shift_row in range(stencil):
        for shift_col in range(stencil):
            segment = extended[
                shift_row : shift_row + row_count, shift_col : shift_col + lon_count, :
            ]
            factor = coef_table[:, shift_row, :, shift_col]
            summed = summed + factor[:, None, :, None] * segment[:, :, None, :].astype(jnp.float32)
    return summed


def spread_back(extended, coef_table):
    row_count = extended.shape[0] - 2 * HALO
    lon_count = extended.shape[1] - 2 * HALO
    stencil = 2 * HALO + 1
    summed = jnp.zeros((row_count, lon_count, extended.shape[3]), jnp.float32)
    for shift_row in range(stencil):
        for shift_col in range(stencil):
            base_row = 2 * HALO - shift_row
            base_col = 2 * HALO - shift_col
            segment = extended[base_row : base_row + row_count, base_col : base_col + lon_count]
            factor = coef_table[base_row : base_row + row_count, shift_row, :, shift_col]
            summed = summed + jnp.sum(
                factor[:, None, :, None] * segment.astype(jnp.float32), axis=2
            )
    return summed


def border(state_field):
    return padded(state_field, (("lat", 0), ("lon", 1)), HALO)


def body(activations, cotangent, w_first, w_second, offsets, basis, live, taps):
    row_count, lon_count, local_ch = activations.shape
    channels = w_first.shape[1]
    lat_count = offsets.shape[0]
    full_table = coefficients(offsets, basis, live, taps)
    first_row = lax.axis_index("lat") * row_count
    own_table = lax.dynamic_slice_in_dim(full_table, first_row, row_count, 0)
    cycle_rows = (first_row - HALO + jnp.arange(row_count + 2 * HALO, dtype=jnp.int32)) % lat_count
    near_table = jnp.take(full_table, cycle_rows, axis=0)
    weights = (w_first, w_second)
    saved = []
    state_field = activations
    for layer_index in range(2):
        weight = weights[layer_index]
        extended = border(state_field)
        widened = lax.all_gather(extended, "chan", axis=2, tiled=True)
        gathered = spread(widened, own_table).astype(jnp.bfloat16)
        flat_pre = jnp.dot(
            gathered.reshape(row_count * lon_count, KB * channels),
            weight.reshape(KB * channels, local_ch),
            preferred_element_type=jnp.float32,
        )
        mixed_pre = flat_pre.reshape(row_count, lon_count, local_ch)
        saved.append((gathered, mixed_pre))
        state_field = (state_field.astype(jnp.float32) + jax.nn.gelu(mixed_pre)).astype(
            jnp.bfloat16
        )
    full_first, full_second = (
        lax.all_gather(w_first, "chan", axis=2, tiled=True),
        lax.all_gather(w_second, "chan", axis=2, tiled=True),
    )
    full_weights = (full_first, full_second)
    chan_start = lax.axis_index("chan") * local_ch
    upstream = cotangent
    grad_sums = [None, None]
    grad_input = None
    for layer_index in (1, 0):
        gathered, mixed_pre = saved[layer_index]
        gelu_grad = jax.vjp(jax.nn.gelu, mixed_pre)[1](upstream.astype(jnp.float32))[0]
        dpre = gelu_grad.astype(jnp.bfloat16)
        local_grad = lax.dot_general(
            gathered.reshape(row_count * lon_count, KB * channels),
            dpre.reshape(row_count * lon_count, local_ch),
            (((0,), (0,)), ((), ())),
            preferred_element_type=jnp.float32,
        )
        local_grad = local_grad.reshape(KB, channels, local_ch)
        grad_sums[layer_index] = lax.psum(local_grad, ("lat", "lon"))
        own_rows = lax.dynamic_slice_in_dim(full_weights[layer_index], chan_start, local_ch, 1)
        dpre_all = lax.all_gather(dpre, "chan", axis=2, tiled=True)
        dfilter = jnp.einsum(
            "xo,kco->xkc",
            dpre_all.reshape(row_count * lon_count, channels),
            own_rows,
            preferred_element_type=jnp.float32,
        )
        dfilter = dfilter.reshape(row_count, lon_count, KB, local_ch).astype(jnp.bfloat16)
        adjoint = spread_back(border(dfilter), near_table)
        combined = upstream.astype(jnp.float32) + adjoint
        if layer_index == 1:
            upstream = combined.astype(jnp.bfloat16)
        else:
            grad_input = combined
    return (state_field, grad_input, grad_sums[0], grad_sums[1])


def solution(mesh):
    return jax.shard_map(
        body,
        mesh=mesh,
        in_specs=(
            P(("groups", "lat"), "lon", "chan"),
            P(("groups", "lat"), "lon", "chan"),
            P(None, None, "chan"),
            P(None, None, "chan"),
            P(),
            P(),
            P(),
            P(),
        ),
        out_specs=(
            P(("groups", "lat"), "lon", "chan"),
            P(("groups", "lat"), "lon", "chan"),
            P("groups", None, "chan"),
            P("groups", None, "chan"),
        ),
        check_vma=False,
    )
```

profile of v0, /device:TPU:0, one launch (start us, length us, event | category | flops | bytes accessed | tf_op | source)
XLA Modules:
  0.0 198.0 jit_solution(15752976534213190520)
XLA Ops:
  7.3 0.7 all-gather.3.cloned.1.call-update
  8.0 0.8 fusion.41
  8.8 3.1 %collective-permute-start = (bf16[1,96,256]{2,1,0:T(8,128)(2,1)S(1)}, bf16[1,96,256]{2,1,0:T(8,128)(2,1)S(1)}, u32[]{:S(2)}, u32[]{:S(2)}) collective-permute-start(bf16[1,96,256]{2,1,0:T(8,128)(2,1)S(1)} %get-tuple-element.74), channel_id=1, source_target_pairs={{0,4},{4,8},{8,12},{12,0},{1,5},{5,9},{9,13},{13,1},{2,6},{6,10},{... | collective-permute-start | bytes 147464 | tf_op jit(solution)/shard_map/ppermute | solution.py:17
  11.9 2.1 %collective-permute-start.1 = (bf16[1,96,256]{2,1,0:T(8,128)(2,1)S(1)}, bf16[1,96,256]{2,1,0:T(8,128)(2,1)S(1)}, u32[]{:S(2)}, u32[]{:S(2)}) collective-permute-start(bf16[1,96,256]{2,1,0:T(8,128)(2,1)S(1)} %get-tuple-element.73), channel_id=1, source_target_pairs={{4,0},{8,4},{12,8},{0,12},{5,1},{9,5},{13,9},{1,13},{6,2},{10,6},{... | collective-permute-start | bytes 147464 | tf_op jit(solution)/shard_map/ppermute | solution.py:19
  14.3 0.1 constant_dynamic-slice_fusion.7
  14.4 1.7 collective-permute-done
  16.1 0.4 collective-permute-done.1
  16.6 0.5 collective-permute-start.3
  17.1 0.1 copy.41
  17.3 0.1 copy.30
  17.3 0.1 copy.31
  17.4 0.1 copy.32
  17.7 0.1 copy.35
  18.1 0.6 gather_fusion
  18.8 17.1 %all_gather.18 = bf16[6,98,512]{2,1,0:T(8,128)(2,1)S(1)} all-gather(bf16[6,98,256]{2,1,0:T(8,128)(2,1)S(1)} %pad_maximum_fusion.6), channel_id=1, replica_groups=mesh['groups'=2,'lat'=4,'chan'=2,'lon'=2] {'chan'}, dimensions={2}, use_global_device_ids=true | all-gather | bytes 903168 | tf_op jit(solution)/shard_map/all_gather | solution.py:91
  35.9 0.9 slice_convert_fusion.17
  36.8 4.3 %add_convert_fusion.1 = bf16[4,96,3,512]{3,2,1,0:T(4,128)(2,1)S(1)} fusion(f32[4,96,512]{2,1,0:T(8,128)S(1)} %get-tuple-element.53, f32[4,3]{1,0:T(4,128)S(1)} %bitcast.89, f32[4,96,512]{2,1,0:T(8,128)S(1)} %get-tuple-element.54, f32[4,3]{1,0:T(4,128)S(1)} %bitcast.87, f32[4,96,512]{2,1,0:T(8,128)S(1)} %get-tuple-element.55, f32[4,3]{1,0:T(4,128)S(1)} %bitcast.85, ...), kind=kLoop, calls=%fused_computation.2 | loop fusion | flops 10616832 | bytes 8257968 | tf_op jit(solution)/shard_map/convert_element_type | solution.py:92
  41.2 0.6 add_convert_fusion.3
  41.8 1.1 collective-permute-start.4
  42.8 2.8 %collective-permute-start.5 = (bf16[1,96,256]{2,1,0:T(8,128)(2,1)S(1)}, bf16[1,96,256]{2,1,0:T(8,128)(2,1)S(1)}, u32[]{:S(2)}, u32[]{:S(2)}) collective-permute-start(bf16[1,96,256]{2,1,0:T(8,128)(2,1)S(1)} %get-tuple-element.72), channel_id=1, source_target_pairs={{4,0},{8,4},{12,8},{0,12},{5,1},{9,5},{13,9},{1,13},{6,2},{10,6},{... | collective-permute-start | bytes 147464 | tf_op jit(solution)/shard_map/ppermute | solution.py:19
  45.7 2.3 %collective-permute-done.4 = bf16[1,96,256]{2,1,0:T(8,128)(2,1)S(1)} collective-permute-done((bf16[1,96,256]{2,1,0:T(8,128)(2,1)S(1)}, bf16[1,96,256]{2,1,0:T(8,128)(2,1)S(1)}, u32[]{:S(2)}, u32[]{:S(2)}) %collective-permute-start.4) | collective-permute-done | bytes 49184 | tf_op jit(solution)/shard_map/ppermute | solution.py:17
  48.2 0.5 collective-permute-start.7
  48.7 0.8 slice_reduce_fusion.7
  49.4 0.4 copy.48
  49.8 0.7 copy.42
  50.7 14.4 %all_gather.19 = bf16[6,98,512]{2,1,0:T(8,128)(2,1)S(1)} all-gather(bf16[6,98,256]{2,1,0:T(8,128)(2,1)S(1)} %pad_maximum_fusion.7), channel_id=1, replica_groups=mesh['groups'=2,'lat'=4,'chan'=2,'lon'=2] {'chan'}, dimensions={2}, use_global_device_ids=true | all-gather | bytes 903168 | tf_op jit(solution)/shard_map/all_gather | solution.py:91
  65.1 0.9 slice_convert_fusion.8
  66.0 4.3 %add_convert_fusion = bf16[4,96,3,512]{3,2,1,0:T(4,128)(2,1)S(1)} fusion(f32[4,96,512]{2,1,0:T(8,128)S(1)} %get-tuple-element.44, f32[4,96,512]{2,1,0:T(8,128)S(1)} %get-tuple-element.45, f32[4,96,512]{2,1,0:T(8,128)S(1)} %get-tuple-element.46, f32[4,96,512]{2,1,0:T(8,128)S(1)} %get-tuple-element.47, f32[4,96,512]{2,1,0:T(8,128)S(1)} %get-tuple-element.48, ...), kind=kLoop, calls=%fused_computation.1 | loop fusion | flops 10616832 | bytes 8257968 | tf_op jit(solution)/shard_map/convert_element_type | solution.py:92
  70.4 1.4 copy.49
  71.7 2.4 %copy.43 = bf16[1536,384]{1,0:T(8,128)(2,1)} copy(bf16[1536,384]{0,1:T(8,128)(2,1)} %bitcast.70) | data formatting | bytes 2359296 | tf_op jit(solution)/shard_map/dot_general | solution.py:116
  74.1 2.6 %fusion.21 = (bf16[4,96,256]{2,1,0:T(8,128)(2,1)S(1)}, bf16[4,96,256]{2,1,0:T(8,128)(2,1)}) fusion(bf16[4,96,256]{2,1,0:T(8,128)(2,1)} %param.9, bf16[4,96,256]{2,1,0:T(8,128)(2,1)S(1)} %get-tuple-element.84, bf16[3,512,256]{2,1,0:T(8,128)(2,1)} %param.11, bf16[4,96,3,512]{3,2,1,0:T(4,128)(2,1)S(1)} %add_convert_fusion), kind=kOutput, calls=%fused_computation.64 | convolution fusion | flops 304447488 | bytes 2752512 | tf_op jit(solution)/shard_map/dot_general | solution.py:93
  76.7 6.9 %all_gather.20 = bf16[4,96,512]{2,1,0:T(8,128)(2,1)S(1)} all-gather(bf16[4,96,256]{2,1,0:T(8,128)(2,1)S(1)} %get-tuple-element.65), channel_id=1, replica_groups=mesh['groups'=2,'lat'=4,'chan'=2,'lon'=2] {'chan'}, dimensions={2}, use_global_device_ids=true | all-gather | bytes 589824 | tf_op jit(solution)/shard_map/all_gather | solution.py:125
  83.6 1.6 convolution_convert_fusion.1
  85.3 0.3 collective-permute-start.8
  85.6 3.6 %collective-permute-start.9 = (bf16[1,96,3,256]{3,1,2,0:T(8,128)(2,1)S(1)}, bf16[1,96,3,256]{3,1,2,0:T(8,128)(2,1)S(1)}, u32[]{:S(2)}, u32[]{:S(2)}) collective-permute-start(bf16[1,96,3,256]{3,1,2,0:T(8,128)(2,1)S(1)} %get-tuple-element.64), channel_id=1, source_target_pairs={{4,0},{8,4},{12,8},{0,12},{5,1},{9,5},{13,9},{1,13},{6,2},{10,6},{... | collective-permute-start | bytes 442376 | tf_op jit(solution)/shard_map/ppermute | solution.py:19
  89.2 1.7 fusion.43
  90.9 1.5 collective-permute-done.8
  92.5 0.5 collective-permute-start.11
  93.0 0.4 multiply_reduce_fusion.16
  93.4 0.2 collective-permute-done.10
  93.7 0.2 collective-permute-done.11
  93.8 0.5 pad_maximum_fusion
  94.4 0.4 multiply_reduce_fusion.15
  94.8 0.6 multiply_reduce_fusion.17
  95.4 0.3 copy-done.4
  95.7 0.5 fusion.14
  96.2 8.1 %all_gather.22 = bf16[4,96,512]{2,1,0:T(8,128)(2,1)S(1)} all-gather(bf16[4,96,256]{2,1,0:T(8,128)(2,1)S(1)} %get-tuple-element.33), channel_id=1, replica_groups=mesh['groups'=2,'lat'=4,'chan'=2,'lon'=2] {'chan'}, dimensions={2}, use_global_device_ids=true | all-gather | bytes 589824 | tf_op jit(solution)/shard_map/all_gather | solution.py:125
  104.3 1.7 fusion.42
  106.1 1.6 convolution_convert_fusion
  107.7 2.1 %collective-permute-start.12 = (bf16[1,96,3,256]{3,1,2,0:T(8,128)(2,1)S(1)}, bf16[1,96,3,256]{3,1,2,0:T(8,128)(2,1)S(1)}, u32[]{:S(2)}, u32[]{:S(2)}) collective-permute-start(bf16[1,96,3,256]{3,1,2,0:T(8,128)(2,1)S(1)} %get-tuple-element.61), channel_id=1, source_target_pairs={{0,4},{4,8},{8,12},{12,0},{1,5},{5,9},{9,13},{13,1},{2,6},{6,10},{... | collective-permute-start | bytes 442376 | tf_op jit(solution)/shard_map/ppermute | solution.py:17
  109.8 1.9 collective-permute-start.13
  111.8 4.6 %collective-permute-done.12 = bf16[1,96,3,256]{3,1,2,0:T(8,128)(2,1)S(1)} collective-permute-done((bf16[1,96,3,256]{3,1,2,0:T(8,128)(2,1)S(1)}, bf16[1,96,3,256]{3,1,2,0:T(8,128)(2,1)S(1)}, u32[]{:S(2)}, u32[]{:S(2)}) %collective-permute-start.12) | collective-permute-done | bytes 147488 | tf_op jit(solution)/shard_map/ppermute | solution.py:17
  116.4 4.8 %collective-permute-done.13 = bf16[1,96,3,256]{3,1,2,0:T(8,128)(2,1)S(1)} collective-permute-done((bf16[1,96,3,256]{3,1,2,0:T(8,128)(2,1)S(1)}, bf16[1,96,3,256]{3,1,2,0:T(8,128)(2,1)S(1)}, u32[]{:S(2)}, u32[]{:S(2)}) %collective-permute-start.13) | collective-permute-done | bytes 147488 | tf_op jit(solution)/shard_map/ppermute | solution.py:19
  121.3 0.5 collective-permute-start.15
  121.8 0.4 multiply_reduce_fusion.7
  122.2 0.3 collective-permute-done.14
  122.5 0.2 collective-permute-done.15
  122.7 0.5 pad_maximum_fusion.1
  123.2 0.4 multiply_reduce_fusion.6
  123.6 0.6 multiply_reduce_fusion.8
  124.2 1.0 convert_add_fusion
  125.2 62.4 %all-reduce.3.cloned.1.call-done = (f32[3,512,256]{2,1,0:T(8,128)}, f32[3,512,256]{2,1,0:T(8,128)}) async-done(((f32[3,512,256]{2,1,0:T(8,128)}, f32[3,512,256]{2,1,0:T(8,128)}), (f32[3,512,256]{2,1,0:T(8,128)}, f32[3,512,256]{2,1,0:T(8,128)})) %all-reduce.3.cloned.1.call-update) | async-done | bytes 3145744 | tf_op jit(solution)/shard_map/psum | solution.py:123
  187.6 2.8 %copy.62 = f32[3,512,256]{2,1,0:T(8,128)} copy(f32[3,512,256]{2,1,0:T(8,128)} %get-tuple-element.90) | data formatting | bytes 3145728
  190.3 1.1 copy.63
  (83 shorter events, 1.6 us)
Async XLA Ops:
  7.2 8.9 %copy-start.3 = (bf16[4,96,256]{2,1,0:T(8,128)(2,1)S(1)}, bf16[4,96,256]{2,1,0:T(8,128)(2,1)}, u32[]{:S(2)}) copy-start(bf16[4,96,256]{2,1,0:T(8,128)(2,1)} %param.8) | copy-start | bytes 589828
  7.2 6.9 %copy-start.19 = (s32[16]{0:T(128)S(1)}, s32[16]{0:T(128)}, u32[]{:S(2)}) copy-start(s32[16]{0:T(128)} %param.14) | copy-start | bytes 196
  7.2 6.9 %copy-start.16 = (f32[16,6,3]{0,2,1:T(4,128)S(1)}, f32[16,6,3]{0,2,1:T(4,128)}, u32[]{:S(2)}) copy-start(f32[16,6,3]{0,2,1:T(4,128)} %param.15) | copy-start | bytes 3460
  7.2 6.9 %copy-start.18 = (s32[16,6]{0,1:T(8,128)S(1)}, s32[16,6]{0,1:T(8,128)}, u32[]{:S(2)}) copy-start(s32[16,6]{0,1:T(8,128)} %param.12) | copy-start | bytes 1156
  7.2 6.9 %copy-start.17 = (s32[16,6]{0,1:T(8,128)S(1)}, s32[16,6]{0,1:T(8,128)}, u32[]{:S(2)}) copy-start(s32[16,6]{0,1:T(8,128)} %param.13) | copy-start | bytes 1156
  7.2 76.4 %all-gather.3.cloned.1.call-start = ((), (), s32[]{:S(2)}) async-start(), calls=%async_computation | async-start | bytes 2359296 | tf_op jit(solution)/shard_map/all_gather | solution.py:105
  8.0 98.1 %all-gather.5.cloned.1.call-start = ((), (), s32[]{:S(2)}) async-start(), calls=%async_computation.1 | async-start | bytes 2359296 | tf_op jit(solution)/shard_map/all_gather | solution.py:104
  8.8 7.3 %collective-permute-start = (bf16[1,96,256]{2,1,0:T(8,128)(2,1)S(1)}, bf16[1,96,256]{2,1,0:T(8,128)(2,1)S(1)}, u32[]{:S(2)}, u32[]{:S(2)}) collective-permute-start(bf16[1,96,256]{2,1,0:T(8,128)(2,1)S(1)} %get-tuple-element.74), channel_id=1, source_target_pairs={{0,4},{4,8},{8,12},{12,0},{1,5},{5,9},{9,13},{13,1},{2,6},{6,10},{... | collective-permute-start | bytes 147464 | tf_op jit(solution)/shard_map/ppermute | solution.py:17
  11.9 4.6 %collective-permute-start.1 = (bf16[1,96,256]{2,1,0:T(8,128)(2,1)S(1)}, bf16[1,96,256]{2,1,0:T(8,128)(2,1)S(1)}, u32[]{:S(2)}, u32[]{:S(2)}) collective-permute-start(bf16[1,96,256]{2,1,0:T(8,128)(2,1)S(1)} %get-tuple-element.73), channel_id=1, source_target_pairs={{4,0},{8,4},{12,8},{0,12},{5,1},{9,5},{13,9},{1,13},{6,2},{10,6},{... | collective-permute-start | bytes 147464 | tf_op jit(solution)/shard_map/ppermute | solution.py:19
  14.0 173.6 %all-reduce.3.cloned.1.call-start = ((), (), s32[]{:S(2)}) async-start(), calls=%async_computation.2 | async-start | bytes 6291456 | tf_op jit(solution)/shard_map/psum | solution.py:123
  16.5 2.2 %collective-permute-start.2 = (bf16[6,1,256]{2,1,0:T(2,128)(2,1)S(1)}, bf16[6,1,256]{2,1,0:T(2,128)(2,1)S(1)}, u32[]{:S(2)}, u32[]{:S(2)}) collective-permute-start(bf16[6,1,256]{2,1,0:T(2,128)(2,1)S(1)} %get-tuple-element.69), channel_id=1, source_target_pairs={{0,1},{1,0},{2,3},{3,2},{4,5},{5,4},{6,7},{7,6},{8,9},{9,8},{10,11... | collective-permute-start | bytes 9224 | tf_op jit(solution)/shard_map/ppermute | solution.py:17
  16.6 2.1 %collective-permute-start.3 = (bf16[6,1,256]{2,1,0:T(2,128)(2,1)S(1)}, bf16[6,1,256]{2,1,0:T(2,128)(2,1)S(1)}, u32[]{:S(2)}, u32[]{:S(2)}) collective-permute-start(bf16[6,1,256]{2,1,0:T(2,128)(2,1)S(1)} %get-tuple-element.70), channel_id=1, source_target_pairs={{1,0},{0,1},{3,2},{2,3},{5,4},{4,5},{7,6},{6,7},{9,8},{8,9},{11,10... | collective-permute-start | bytes 9224 | tf_op jit(solution)/shard_map/ppermute | solution.py:19
  17.9 18.9 %copy-start.10 = (f32[4,1,3,1]{2,0,3,1:T(4,128)}, f32[4,1,3,1]{2,0,3,1:T(4,128)S(1)}, u32[]{:S(2)}) copy-start(f32[4,1,3,1]{2,0,3,1:T(4,128)S(1)} %copy.36) | copy-start | bytes 148
  18.0 18.8 %copy-start.12 = (f32[4,1,3,1]{2,0,3,1:T(4,128)}, f32[4,1,3,1]{2,0,3,1:T(4,128)S(1)}, u32[]{:S(2)}) copy-start(f32[4,1,3,1]{2,0,3,1:T(4,128)S(1)} %copy.37) | copy-start | bytes 148
  18.1 18.7 %copy-start.14 = (f32[4,1,3,1]{2,0,3,1:T(4,128)}, f32[4,1,3,1]{2,0,3,1:T(4,128)S(1)}, u32[]{:S(2)}) copy-start(f32[4,1,3,1]{2,0,3,1:T(4,128)S(1)} %copy.38) | copy-start | bytes 148
  36.8 4.4 %copy-start.2 = (bf16[3,512,256]{2,1,0:T(8,128)(2,1)S(1)}, bf16[3,512,256]{2,1,0:T(8,128)(2,1)}, u32[]{:S(2)}) copy-start(bf16[3,512,256]{2,1,0:T(8,128)(2,1)} %param.10) | copy-start | bytes 2359300
  41.8 6.3 %collective-permute-start.4 = (bf16[1,96,256]{2,1,0:T(8,128)(2,1)S(1)}, bf16[1,96,256]{2,1,0:T(8,128)(2,1)S(1)}, u32[]{:S(2)}, u32[]{:S(2)}) collective-permute-start(bf16[1,96,256]{2,1,0:T(8,128)(2,1)S(1)} %get-tuple-element.71), channel_id=1, source_target_pairs={{0,4},{4,8},{8,12},{12,0},{1,5},{5,9},{9,13},{13,1},{2,6},{6,10},{... | collective-permute-start | bytes 147464 | tf_op jit(solution)/shard_map/ppermute | solution.py:17
  42.8 5.2 %collective-permute-start.5 = (bf16[1,96,256]{2,1,0:T(8,128)(2,1)S(1)}, bf16[1,96,256]{2,1,0:T(8,128)(2,1)S(1)}, u32[]{:S(2)}, u32[]{:S(2)}) collective-permute-start(bf16[1,96,256]{2,1,0:T(8,128)(2,1)S(1)} %get-tuple-element.72), channel_id=1, source_target_pairs={{4,0},{8,4},{12,8},{0,12},{5,1},{9,5},{13,9},{1,13},{6,2},{10,6},{... | collective-permute-start | bytes 147464 | tf_op jit(solution)/shard_map/ppermute | solution.py:19
  48.1 2.5 %collective-permute-start.6 = (bf16[6,1,256]{2,1,0:T(2,128)(2,1)S(1)}, bf16[6,1,256]{2,1,0:T(2,128)(2,1)S(1)}, u32[]{:S(2)}, u32[]{:S(2)}) collective-permute-start(bf16[6,1,256]{2,1,0:T(2,128)(2,1)S(1)} %get-tuple-element.67), channel_id=1, source_target_pairs={{0,1},{1,0},{2,3},{3,2},{4,5},{5,4},{6,7},{7,6},{8,9},{9,8},{10,11... | collective-permute-start | bytes 9224 | tf_op jit(solution)/shard_map/ppermute | solution.py:17
  48.2 2.4 %collective-permute-start.7 = (bf16[6,1,256]{2,1,0:T(2,128)(2,1)S(1)}, bf16[6,1,256]{2,1,0:T(2,128)(2,1)S(1)}, u32[]{:S(2)}, u32[]{:S(2)}) collective-permute-start(bf16[6,1,256]{2,1,0:T(2,128)(2,1)S(1)} %get-tuple-element.68), channel_id=1, source_target_pairs={{1,0},{0,1},{3,2},{2,3},{5,4},{4,5},{7,6},{6,7},{9,8},{8,9},{11,10... | collective-permute-start | bytes 9224 | tf_op jit(solution)/shard_map/ppermute | solution.py:19
  65.1 0.9 copy-start.11
  65.1 0.9 copy-start.13
  65.1 0.9 copy-start.15
  76.7 12.5 %copy-start = (bf16[1536,384]{1,0:T(8,128)(2,1)S(1)}, bf16[1536,384]{1,0:T(8,128)(2,1)}, u32[]{:S(2)}) copy-start(bf16[1536,384]{1,0:T(8,128)(2,1)} %copy.43) | copy-start | bytes 3538948
  85.3 7.1 %collective-permute-start.8 = (bf16[1,96,3,256]{3,1,2,0:T(8,128)(2,1)S(1)}, bf16[1,96,3,256]{3,1,2,0:T(8,128)(2,1)S(1)}, u32[]{:S(2)}, u32[]{:S(2)}) collective-permute-start(bf16[1,96,3,256]{3,1,2,0:T(8,128)(2,1)S(1)} %get-tuple-element.63), channel_id=1, source_target_pairs={{0,4},{4,8},{8,12},{12,0},{1,5},{5,9},{9,13},{13,1},{2,6},{6,10},{... | collective-permute-start | bytes 442376 | tf_op jit(solution)/shard_map/ppermute | solution.py:17
  85.6 6.8 %collective-permute-start.9 = (bf16[1,96,3,256]{3,1,2,0:T(8,128)(2,1)S(1)}, bf16[1,96,3,256]{3,1,2,0:T(8,128)(2,1)S(1)}, u32[]{:S(2)}, u32[]{:S(2)}) collective-permute-start(bf16[1,96,3,256]{3,1,2,0:T(8,128)(2,1)S(1)} %get-tuple-element.64), channel_id=1, source_target_pairs={{4,0},{8,4},{12,8},{0,12},{5,1},{9,5},{13,9},{1,13},{6,2},{10,6},{... | collective-permute-start | bytes 442376 | tf_op jit(solution)/shard_map/ppermute | solution.py:19
  89.2 3.8 %copy-start.7 = (f32[4,3]{1,0:T(4,128)S(1)}, f32[4,3]{1,0:T(4,128)}, u32[]{:S(2)}) copy-start(f32[4,3]{1,0:T(4,128)} %get-tuple-element.22) | copy-start | bytes 148
  89.2 3.8 %copy-start.8 = (f32[4,3]{1,0:T(4,128)S(1)}, f32[4,3]{1,0:T(4,128)}, u32[]{:S(2)}) copy-start(f32[4,3]{1,0:T(4,128)} %get-tuple-element.24) | copy-start | bytes 148
  89.2 3.8 %copy-start.9 = (f32[4,3]{1,0:T(4,128)S(1)}, f32[4,3]{1,0:T(4,128)}, u32[]{:S(2)}) copy-start(f32[4,3]{1,0:T(4,128)} %get-tuple-element.27) | copy-start | bytes 148
  92.4 1.3 collective-permute-start.10
  92.5 1.3 collective-permute-start.11
  93.4 0.9 copy-start.5
  93.4 0.9 copy-start.6
  94.8 0.9 copy-start.4
  107.7 8.6 %collective-permute-start.12 = (bf16[1,96,3,256]{3,1,2,0:T(8,128)(2,1)S(1)}, bf16[1,96,3,256]{3,1,2,0:T(8,128)(2,1)S(1)}, u32[]{:S(2)}, u32[]{:S(2)}) collective-permute-start(bf16[1,96,3,256]{3,1,2,0:T(8,128)(2,1)S(1)} %get-tuple-element.61), channel_id=1, source_target_pairs={{0,4},{4,8},{8,12},{12,0},{1,5},{5,9},{9,13},{13,1},{2,6},{6,10},{... | collective-permute-start | bytes 442376 | tf_op jit(solution)/shard_map/ppermute | solution.py:17
  109.8 11.4 %collective-permute-start.13 = (bf16[1,96,3,256]{3,1,2,0:T(8,128)(2,1)S(1)}, bf16[1,96,3,256]{3,1,2,0:T(8,128)(2,1)S(1)}, u32[]{:S(2)}, u32[]{:S(2)}) collective-permute-start(bf16[1,96,3,256]{3,1,2,0:T(8,128)(2,1)S(1)} %get-tuple-element.62), channel_id=1, source_target_pairs={{4,0},{8,4},{12,8},{0,12},{5,1},{9,5},{13,9},{1,13},{6,2},{10,6},{... | collective-permute-start | bytes 442376 | tf_op jit(solution)/shard_map/ppermute | solution.py:19
  121.2 1.3 collective-permute-start.14
  121.3 1.3 collective-permute-start.15
  187.6 2.8 %copy-start.1 = (f32[3,512,256]{2,1,0:T(8,128)S(1)}, f32[3,512,256]{2,1,0:T(8,128)}, u32[]{:S(2)}) copy-start(f32[3,512,256]{2,1,0:T(8,128)} %get-tuple-element.91) | copy-start | bytes 4718596
Sparse Core Ops, SparseCore 0:
  9.6 36.4 all-gather.2
  47.6 30.2 all-gather.4
  106.2 81.3 all-reduce.2
where the time goes:
time: 198 us
  waiting for transfers between devices  79.3 us (40%)
  blocking collectives  46.5 us (23%)
  starting transfers between devices  19.3 us (10%)
  other arithmetic  16.4 us (8%)
  between operations  14.3 us (7%)
  local copies, waits for them, and re-layouts  12.5 us (6%)
  matrix products  9.84 us (5%)
    psum x1, waiting for transfers between devices, body(): grad_sums[layer_index] = lax.psum(local_grad, ('lat', 'lon'))  62.4 us
    all_gather x2, blocking collectives, body(): widened = lax.all_gather(extended, 'chan', axis=2, tiled=True)  31.5 us
    all_gather x2, blocking collectives, body(): dpre_all = lax.all_gather(dpre, 'chan', axis=2, tiled=True)  15 us
    ppermute x8, starting transfers between devices, padded(): lax.ppermute(head, axis, [((i + 1) % count, i) for i in range(count)])  11.5 us
    ppermute x8, waiting for transfers between devices, padded(): lax.ppermute(tail, axis, [(i, (i + 1) % count) for i in range(count)])  10.4 us
    convert_element_type x2, other arithmetic, body(): gathered = spread(widened, own_table).astype(jnp.bfloat16)  8.69 us
    ppermute x8, starting transfers between devices, padded(): lax.ppermute(tail, axis, [(i, (i + 1) % count) for i in range(count)])  7.64 us
    unnamed x47, local copies, waits for them, and re-layouts  6.08 us
  transfers between devices with their start and end apart: 19, of which 11 were waited for; matrix products, arithmetic and copies ran while one was open for 17% of the time, Pallas kernels for 0%

commit v1 on v0

v1 whole, which is shorter than its diff:
```python
import functools
import math

import jax
import jax.numpy as jnp
from jax import lax
from jax.experimental import pallas as pl
from jax.experimental.pallas import tpu as pltpu
from jax.sharding import PartitionSpec as P

KB = 3
HALO = 1
EDGE = 16
MESH = pl.DeviceIdType.MESH
BF16 = jnp.bfloat16
F32 = jnp.float32
GELU_C = math.sqrt(2.0 / math.pi)
GELU_A = 0.044715


def coefficients(offsets, basis, live, taps):
    stencil = 2 * HALO + 1
    slot_count = offsets.shape[1]
    in_use = jnp.arange(slot_count)[None, :] < live[:, None]
    row_hit = (offsets[:, :, None] == (jnp.arange(stencil) - HALO)[None, None, :]) & in_use[
        :, :, None
    ]
    kind_hit = basis[:, :, None] == jnp.arange(KB)[None, None, :]
    chosen = row_hit[:, :, :, None] & kind_hit[:, :, None, :]
    return jnp.sum(
        jnp.where(chosen[..., None], taps[:, :, None, None, :], jnp.float32(0.0)), axis=1
    )


def gelu(x):
    th = jnp.tanh(GELU_C * (x + GELU_A * (x * x * x)))
    return 0.5 * x * (1.0 + th)


def gelu_slope(x):
    sq = x * x
    th = jnp.tanh(GELU_C * (x + GELU_A * (sq * x)))
    return 0.5 * (1.0 + th) + (0.5 * x) * (1.0 - th * th) * (
        GELU_C * (1.0 + (3.0 * GELU_A) * sq)
    )


def kernel(
    sizes, tab, act, cot, w1, w2, mixed, gin, g1, g2,
    ext, wb, band, v1, v2, vb, pre1, back, part, rs_out, rs_in, tot,
    s_right, r_right, s_left, r_left, ag_out, ag_in,
    x_send, x_recv, w_send, w_recv, f_send, f_recv, rs_send, rs_recv, c_send, c_recv,
    ag_send, ag_recv,
):
    nlat, nchan, nlon, chunks = sizes
    rows, cols, width = act.shape
    channels = nchan * width
    wide = cols + 2 * EDGE
    lat, chan, lon = lax.axis_index("lat"), lax.axis_index("chan"), lax.axis_index("lon")
    has_up, has_down = lat > 0, lat < nlat - 1
    mid = pl.ds(EDGE, cols)

    @pl.when(lat == 0)
    def _():
        ext[:, :, 0] = jnp.zeros(ext.shape[:2] + ext.shape[3:], BF16)

    @pl.when(lat == nlat - 1)
    def _():
        ext[:, :, rows + 1] = jnp.zeros(ext.shape[:2] + ext.shape[3:], BF16)

    barrier = pltpu.get_barrier_semaphore()

    def chan_at(step):
        return lax.rem(chan + step + nchan, nchan)

    def lon_at(step):
        return lax.rem(lon + step + nlon, nlon)

    for step in range(1, nchan):
        pl.semaphore_signal(barrier, inc=1, device_id={"chan": chan_at(step)}, device_id_type=MESH)
    for step in range(1, nlon):
        pl.semaphore_signal(barrier, inc=1, device_id={"lon": lon_at(step)}, device_id_type=MESH)

    @pl.when(has_up)
    def _():
        for step in range(nchan):
            pl.semaphore_signal(
                barrier, inc=1, device_id={"lat": lat - 1, "chan": chan_at(step)}, device_id_type=MESH
            )

    @pl.when(has_down)
    def _():
        for step in range(nchan):
            pl.semaphore_signal(
                barrier, inc=1, device_id={"lat": lat + 1, "chan": chan_at(step)}, device_id_type=MESH
            )

    gap = (
        lax.broadcasted_iota(jnp.int32, (cols, wide), 1)
        - lax.broadcasted_iota(jnp.int32, (cols, wide), 0)
        - (EDGE - 1)
    )
    masks = [jnp.where(gap == t, 1.0, 0.0).astype(F32) for t in range(3)]
    def build_band(which):
        for i in range(rows):
            for k in range(KB):
                for e in range(3):
                    if which == 0:
                        c = [tab[i + 1, e * 9 + k * 3 + t] for t in range(3)]
                    else:
                        c = [tab[i + e, (2 - e) * 9 + k * 3 + 2 - t] for t in range(3)]
                    block = masks[0] * c[0] + masks[1] * c[1] + masks[2] * c[2]
                    band[which, i, k * cols:(k + 1) * cols, e * wide:(e + 1) * wide] = block.astype(BF16)

    sides = jnp.minimum(lat, 1) + jnp.minimum(nlat - 1 - lat, 1)
    pl.semaphore_wait(barrier, nchan + nlon - 2 + nchan * sides)

    def remote(src, dst, send, recv, where):
        return pltpu.make_async_remote_copy(
            src_ref=src, dst_ref=dst, send_sem=send, recv_sem=recv,
            device_id=where, device_id_type=MESH,
        )

    def block_copy(x, step, slot):
        return remote(
            ext.at[x, slot, 1:rows + 1, mid], ext.at[x, slot, 1:rows + 1, mid],
            x_send.at[x, step], x_recv.at[x, step], {"chan": chan_at(step)},
        )

    def row_copy(x, step, slot, down):
        src, dst = (rows, 0) if down else (1, rows + 1)
        sem = (2 if down else 1) * nchan + step
        return remote(
            ext.at[x, slot, pl.ds(src, 1), mid], ext.at[x, slot, pl.ds(dst, 1), mid],
            x_send.at[x, sem], x_recv.at[x, sem],
            {"lat": lat + 1 if down else lat - 1, "chan": chan_at(step)},
        )

    def col_copy(x, right):
        src, dst = (cols, 0) if right else (EDGE, EDGE + cols)
        sem = 3 * nchan + (1 if right else 0)
        return remote(
            ext.at[x, :, :, pl.ds(src, EDGE)], ext.at[x, :, :, pl.ds(dst, EDGE)],
            x_send.at[x, sem], x_recv.at[x, sem], {"lon": lon_at(1 if right else -1)},
        )

    def on_rows(x, what, own):
        @pl.when(has_down)
        def _():
            for step in range(nchan):
                if own:
                    what(row_copy(x, step, chan, True))
                else:
                    what(row_copy(x, step, chan_at(-step), False))

        @pl.when(has_up)
        def _():
            for step in range(nchan):
                if own:
                    what(row_copy(x, step, chan, False))
                else:
                    what(row_copy(x, step, chan_at(-step), True))

    def start_exchange(x):
        on_rows(x, lambda c: c.start(), True)
        for step in range(1, nchan):
            block_copy(x, step, chan).start()

    def wait_row(x, step, slot, down):
        dst = 0 if down else rows + 1
        sem = (2 if down else 1) * nchan + step
        remote(
            ext.at[x, slot, pl.ds(dst, 1), mid], ext.at[x, slot, pl.ds(dst, 1), mid],
            x_send.at[x, sem], x_recv.at[x, sem],
            {"lat": lat - 1 if down else lat + 1, "chan": chan_at(-step)},
        ).wait_recv()

    def finish_exchange(x):
        @pl.when(has_up)
        def _():
            for step in range(nchan):
                wait_row(x, step, chan_at(-step), True)

        @pl.when(has_down)
        def _():
            for step in range(nchan):
                wait_row(x, step, chan_at(-step), False)

        for step in range(1, nchan):
            block_copy(x, step, chan_at(-step)).wait_recv()
        col_copy(x, True).start()
        col_copy(x, False).start()
        col_copy(x, True).wait_recv()
        col_copy(x, False).wait_recv()

    def end_exchange(x):
        on_rows(x, lambda c: c.wait_send(), True)
        for step in range(1, nchan):
            block_copy(x, step, chan).wait_send()
        col_copy(x, True).wait_send()
        col_copy(x, False).wait_send()

    half_w = width // nlon
    weights = (w1, w2)

    def weight_copy(which, step, peer, slot):
        return remote(
            weights[which].at[:, pl.ds(pl.multiple_of(peer * width + lon * half_w, half_w), half_w)],
            wb.at[which, :, pl.ds(pl.multiple_of(lon * half_w, half_w), half_w),
                  pl.ds(pl.multiple_of(slot * width, width), width)],
            w_send.at[which, step], w_recv.at[which, step], {"chan": chan_at(step)},
        )

    def forward_copy(which, step, hop, owner):
        at = (
            which, slice(None), pl.ds(pl.multiple_of(owner * half_w, half_w), half_w),
            pl.ds(pl.multiple_of(chan_at(-step) * width, width), width),
        )
        return remote(
            wb.at[at], wb.at[at], f_send.at[which, step, hop], f_recv.at[which, step, hop],
            {"lon": lon_at(hop)},
        )

    def apply_filter(which, x, out):
        for i in range(rows):
            for slot in range(nchan):
                seen = ext[x, slot, i:i + 3].reshape(3 * wide, width)
                got = jnp.dot(band[which, i], seen, preferred_element_type=F32).astype(BF16)
                for k in range(KB):
                    out[i * cols:(i + 1) * cols,
                        k * channels + slot * width:k * channels + (slot + 1) * width] = got[
                            k * cols:(k + 1) * cols]

    def put(x, value):
        ext[x, chan, 1:rows + 1, mid] = value.reshape(rows, cols, width)

    def mix_back(which):
        total = None
        for k in range(KB):
            term = lax.dot_general(
                vb[:, k * channels:(k + 1) * channels], wb[which, k],
                (((1,), (1,)), ((), ())), preferred_element_type=F32,
            )
            total = term if total is None else total + term
        return total

    full_rows = KB * channels
    share = full_rows // nlon
    piece = share // chunks

    def rs_copy(g, step):
        return remote(
            rs_out.at[g, step - 1], rs_in.at[g, step - 1], rs_send.at[g, step - 1],
            rs_recv.at[g, step - 1], {"lon": lon_at(step)},
        )

    def weight_gradient(g, v, dpre):
        for k in range(KB):
            part[g, k * channels:(k + 1) * channels] = lax.dot_general(
                v[:, k * channels:(k + 1) * channels], dpre,
                (((0,), (0,)), ((), ())), preferred_element_type=F32,
            )
        for step in range(1, nlon):
            rs_out[g, step - 1] = part[
                g, pl.ds(pl.multiple_of(lon_at(step) * share, share), share)].astype(BF16)
            rs_copy(g, step).start()

    def chain_copy(g, j, right):
        out, into = (s_right, r_right) if right else (s_left, r_left)
        side = 0 if right else 1
        return remote(
            out.at[g, j], into.at[g, j], c_send.at[g, side, j], c_recv.at[g, side, j],
            {"lat": lat + 1 if right else lat - 1},
        )

    def chain_wait(g, j, right):
        into = r_right if right else r_left
        side = 0 if right else 1
        remote(
            into.at[g, j], into.at[g, j], c_send.at[g, side, j], c_recv.at[g, side, j],
            {"lat": lat - 1 if right else lat + 1},
        ).wait_recv()

    def ag_copy(g, j, step):
        return remote(
            ag_out.at[g, j], ag_in.at[g, step - 1, j], ag_send.at[g, step - 1, j],
            ag_recv.at[g, step - 1, j], {"lon": lon_at(step)},
        )

    def chain(g, out):
        for step in range(1, nlon):
            rs_copy(g, step).wait_recv()
        own = part[g, pl.ds(pl.multiple_of(lon * share, share), share)]
        for step in range(1, nlon):
            own = own + rs_in[g, step - 1].astype(F32)
        tot[g] = own.reshape(chunks, piece, width)
        rest = nlat - 1 - lat
        late = jnp.maximum(lat, rest)

        def tick(time, carry):
            j_right = time - lat
            j_left = time - rest
            j_done = time - late

            @pl.when((j_right >= 0) & (j_right < chunks) & (lat == 0))
            def _():
                s_right[g, j_right] = tot[g, j_right].astype(BF16)

            @pl.when((j_right >= 0) & (j_right < chunks) & (lat > 0))
            def _():
                chain_wait(g, j_right, True)
                s_right[g, j_right] = (tot[g, j_right] + r_right[g, j_right].astype(F32)).astype(BF16)

            @pl.when((j_right >= 0) & (j_right < chunks) & has_down)
            def _():
                chain_copy(g, j_right, True).start()

            @pl.when((j_left >= 0) & (j_left < chunks) & (rest == 0))
            def _():
                s_left[g, j_left] = tot[g, j_left].astype(BF16)

            @pl.when((j_left >= 0) & (j_left < chunks) & (rest > 0))
            def _():
                chain_wait(g, j_left, False)
                s_left[g, j_left] = (tot[g, j_left] + r_left[g, j_left].astype(F32)).astype(BF16)

            @pl.when((j_left >= 0) & (j_left < chunks) & has_up)
            def _():
                chain_copy(g, j_left, False).start()

            @pl.when((j_done >= 0) & (j_done < chunks))
            def _():
                @pl.when(has_up)
                def _():
                    tot[g, j_done] = tot[g, j_done] + r_right[g, j_done].astype(F32)

                @pl.when(has_down)
                def _():
                    tot[g, j_done] = tot[g, j_done] + r_left[g, j_done].astype(F32)

                ag_out[g, j_done] = tot[g, j_done].astype(BF16)
                for step in range(1, nlon):
                    ag_copy(g, j_done, step).start()

            return carry

        lax.fori_loop(0, nlat - 1 + chunks, tick, 0)
        out[pl.ds(pl.multiple_of(lon * share, share), share)] = tot[g].reshape(share, width)

    def chain_end(g, out):
        def settle(j, carry):
            for step in range(1, nlon):
                ag_copy(g, j, step).wait_recv()
                ag_copy(g, j, step).wait_send()

            @pl.when(has_down)
            def _():
                chain_copy(g, j, True).wait_send()

            @pl.when(has_up)
            def _():
                chain_copy(g, j, False).wait_send()

            return carry

        lax.fori_loop(0, chunks, settle, 0)
        for step in range(1, nlon):
            out[pl.ds(pl.multiple_of(lon_at(-step) * share, share), share)] = (
                ag_in[g, step - 1].reshape(share, width).astype(F32)
            )
            rs_copy(g, step).wait_send()

    put(0, act[...])
    start_exchange(0)
    for which in (1, 0):
        for step in range(1, nchan):
            weight_copy(which, step, chan_at(step), chan).start()
    build_band(0)
    build_band(1)
    for which in (1, 0):
        wb[which, :, :, pl.ds(pl.multiple_of(chan * width, width), width)] = weights[which][
            :, pl.ds(pl.multiple_of(chan * width, width), width)]
    finish_exchange(0)
    apply_filter(0, 0, v1)
    first = jnp.dot(v1[...], w1[...].reshape(full_rows, width), preferred_element_type=F32)
    pre1[...] = first
    hidden = (act[...].reshape(rows * cols, width).astype(F32) + gelu(first)).astype(BF16)
    put(1, hidden)
    start_exchange(1)
    for which in (1, 0):
        for step in range(1, nchan):
            weight_copy(which, step, chan, chan_at(-step)).wait_recv()
            for hop in range(1, nlon):
                forward_copy(which, step, hop, lon).start()
    finish_exchange(1)
    apply_filter(0, 1, v2)
    second = jnp.dot(v2[...], w2[...].reshape(full_rows, width), preferred_element_type=F32)
    upstream = cot[...].reshape(rows * cols, width).astype(F32)
    dpre2 = (upstream * gelu_slope(second)).astype(BF16)
    put(2, dpre2)
    start_exchange(2)
    held = ext[1, chan, 1:rows + 1, mid].reshape(rows * cols, width).astype(F32)
    mixed[...] = (held + gelu(second)).astype(BF16).reshape(rows, cols, width)
    weight_gradient(0, v2, dpre2)
    for which in (1, 0):
        for step in range(1, nchan):
            for hop in range(1, nlon):
                forward_copy(which, step, hop, lon_at(-hop)).wait_recv()
    finish_exchange(2)
    apply_filter(1, 2, vb)
    back_hidden = (cot[...].reshape(rows * cols, width).astype(F32) + mix_back(1)).astype(BF16)
    back[...] = back_hidden
    dpre1 = (back_hidden.astype(F32) * gelu_slope(pre1[...])).astype(BF16)
    put(3, dpre1)
    start_exchange(3)
    weight_gradient(1, v1, dpre1)
    chain(0, g2)
    finish_exchange(3)
    apply_filter(1, 3, vb)
    gin[...] = (back[...].astype(F32) + mix_back(0)).reshape(rows, cols, width)
    chain(1, g1)
    chain_end(0, g2)
    chain_end(1, g1)
    for x in range(4):
        end_exchange(x)
    for which in (1, 0):
        for step in range(1, nchan):
            weight_copy(which, step, chan_at(step), chan).wait_send()
            for hop in range(1, nlon):
                forward_copy(which, step, hop, lon).wait_send()


def body(sizes, activations, cotangent, w_first, w_second, offsets, basis, live, taps):
    nlat, nchan, nlon, chunks = sizes
    rows, cols, width = activations.shape
    channels = w_first.shape[1]
    wide = cols + 2 * EDGE
    table = coefficients(offsets, basis, live, taps).reshape(offsets.shape[0], 9 * KB)
    table = jnp.pad(table, ((HALO, HALO), (0, 0)))
    near = lax.dynamic_slice_in_dim(table, lax.axis_index("lat") * rows, rows + 2 * HALO, 0)
    full_rows = KB * channels
    share = full_rows // nlon
    piece = share // chunks
    cells = rows * cols
    dma = pltpu.SemaphoreType.DMA
    vmem = pl.BlockSpec(memory_space=pltpu.VMEM)
    slots = 3 * nchan + 2
    mixed, gin, g1, g2 = pl.pallas_call(
        functools.partial(kernel, sizes),
        out_shape=(
            jax.ShapeDtypeStruct((rows, cols, width), BF16),
            jax.ShapeDtypeStruct((rows, cols, width), F32),
            jax.ShapeDtypeStruct((full_rows, width), F32),
            jax.ShapeDtypeStruct((full_rows, width), F32),
        ),
        in_specs=[pl.BlockSpec(memory_space=pltpu.SMEM)] + [vmem] * 4,
        out_specs=(vmem,) * 4,
        scratch_shapes=[
            pltpu.VMEM((4, nchan, rows + 2, wide, width), BF16),
            pltpu.VMEM((2, KB, width, channels), BF16),
            pltpu.VMEM((2, rows, KB * cols, 3 * wide), BF16),
            pltpu.VMEM((cells, full_rows), BF16),
            pltpu.VMEM((cells, full_rows), BF16),
            pltpu.VMEM((cells, full_rows), BF16),
            pltpu.VMEM((cells, width), F32),
            pltpu.VMEM((cells, width), BF16),
            pltpu.VMEM((2, full_rows, width), F32),
            pltpu.VMEM((2, nlon - 1, share, width), BF16),
            pltpu.VMEM((2, nlon - 1, share, width), BF16),
            pltpu.VMEM((2, chunks, piece, width), F32),
            pltpu.VMEM((2, chunks, piece, width), BF16),
            pltpu.VMEM((2, chunks, piece, width), BF16),
            pltpu.VMEM((2, chunks, piece, width), BF16),
            pltpu.VMEM((2, chunks, piece, width), BF16),
            pltpu.VMEM((2, chunks, piece, width), BF16),
            pltpu.VMEM((2, nlon - 1, chunks, piece, width), BF16),
            dma((4, slots)),
            dma((4, slots)),
            dma((2, nchan)),
            dma((2, nchan)),
            dma((2, nchan, nlon)),
            dma((2, nchan, nlon)),
            dma((2, nlon - 1)),
            dma((2, nlon - 1)),
            dma((2, 2, chunks)),
            dma((2, 2, chunks)),
            dma((2, nlon - 1, chunks)),
            dma((2, nlon - 1, chunks)),
        ],
        compiler_params=pltpu.CompilerParams(
            collective_id=0, has_side_effects=True, vmem_limit_bytes=50 * 1024 * 1024
        ),
    )(near, activations, cotangent, w_first, w_second)
    shape = (KB, channels, width)
    return mixed, gin, g1.reshape(shape), g2.reshape(shape)


def solution(mesh):
    sizes = (mesh.shape["lat"], mesh.shape["chan"], mesh.shape["lon"], 8)
    return jax.shard_map(
        functools.partial(body, sizes),
        mesh=mesh,
        in_specs=(
            P(("groups", "lat"), "lon", "chan"),
            P(("groups", "lat"), "lon", "chan"),
            P(None, None, "chan"),
            P(None, None, "chan"),
            P(),
            P(),
            P(),
            P(),
        ),
        out_specs=(
            P(("groups", "lat"), "lon", "chan"),
            P(("groups", "lat"), "lon", "chan"),
            P("groups", None, "chan"),
            P("groups", None, "chan"),
        ),
        check_vma=False,
    )
```

time: 198 us -> 116 us (0.59)
  Pallas kernels: 0 us -> 104 us
  waiting for transfers between devices: 79.3 us -> 0 us
  blocking collectives: 46.5 us -> 0 us
  starting transfers between devices: 19.3 us -> 0 us
  other arithmetic: 16.4 us -> 1.52 us
  between operations: 14.3 us -> 0.67 us
  matrix products: 9.84 us -> 0 us
  local copies, waits for them, and re-layouts: 12.5 us -> 10.3 us
    pallas_call x0 -> x1, Pallas kernels: none -> 104 us  [body(): pl.pallas_call(functools.partial(kernel, sizes), out_shape=(jax.ShapeDtyp...]
    psum x1 -> x0, waiting for transfers between devices: 62.4 us -> none  [body(): grad_sums[layer_index] = lax.psum(local_grad, ('lat', 'lon'))]
    all_gather x4 -> x0, blocking collectives: 46.5 us -> none  [the longest x2 31.5 us: body(): widened = lax.all_gather(extended, 'chan', axis=2, tiled=True)]
    ppermute x16 -> x0, starting transfers between devices: 19.2 us -> none  [the longest x8 11.5 us: padded(): lax.ppermute(head, axis, [((i + 1) % count, i) for i in range(count)])]
    ppermute x16 -> x0, waiting for transfers between devices: 16.2 us -> none  [the longest x8 10.4 us: padded(): lax.ppermute(tail, axis, [(i, (i + 1) % count) for i in range(count)])]
    convert_element_type x5 -> x0, other arithmetic: 11 us -> none  [the longest x2 8.69 us: body(): gathered = spread(widened, own_table).astype(jnp.bfloat16)]
    dot_general x6 -> x0, matrix products: 9.84 us -> none  [the longest x2 3.41 us: body(): lax.dot_general(gathered.reshape(row_count * lon_count, KB * channels), d...]
    unnamed x47 -> x15, local copies, waits for them, and re-layouts: 6.08 us -> 10.2 us
  transfers between devices with their start and end apart: 19 -> 0, of which waited for: 11 -> 0; matrix products, arithmetic and copies ran while one was open for 17% -> 0% of each run, Pallas kernels for 0% -> 0%
where the time goes in v1:
time: 116 us
  Pallas kernels  104 us (90%)
  local copies, waits for them, and re-layouts  10.3 us (9%)
  other arithmetic  1.52 us (1%)
    pallas_call x1, Pallas kernels, body(): pl.pallas_call(functools.partial(kernel, sizes), out_shape=(jax.ShapeDtyp...  104 us
    unnamed x15, local copies, waits for them, and re-layouts  10.2 us

profile of v1, /device:TPU:0, one launch (start us, length us, event | category | flops | bytes accessed | tf_op | source)
XLA Modules:
  0.0 116.2 jit_solution(6431414115409314907)
XLA Ops:
  0.6 0.7 iota_compare_fusion.1
  1.3 0.8 iota_compare_fusion
  2.1 0.7 copy.19
  2.8 0.1 select_reduce_fusion
  2.9 0.1 copy.20
  3.0 0.0 copy-start
  3.0 1.1 copy-done
  4.1 0.0 copy-start.1
  4.1 1.1 copy-done.1
  5.2 0.0 copy-start.2
  5.2 0.9 copy-done.2
  6.2 0.0 copy-start.3
  6.2 0.9 copy-done.3
  7.1 103.7 %shard_map.111 = (bf16[4,96,256]{2,1,0:T(8,128)(2,1)S(1)}, f32[4,96,256]{2,1,0:T(8,128)S(1)}, f32[1536,256]{1,0:T(8,128)}, f32[1536,256]{1,0:T(8,128)}) custom-call(f32[6,27]{1,0:T(8,128)S(1)} %pad_dynamic-slice_fusion.tab, bf16[4,96,256]{2,1,0:T(8,128)(2,1)S(1)} %copy-done.2, bf16[4,96,256]{2,1,0:T(8,128)(2,1)S(1)} %copy-done.3, ...), custom_call_target="tpu_custom_call" | custom-call | tf_op jit(solution)/shard_map/pallas_call | solution.py:448
  110.8 0.7 copy.25
  111.5 0.7 copy.26
  112.2 0.0 copy-start.4
  112.2 2.8 %copy.27 = f32[3,512,256]{2,1,0:T(8,128)} copy(f32[3,512,256]{2,1,0:T(8,128)} %bitcast.5) | data formatting | bytes 3145728
  115.0 0.0 copy-done.4
  115.0 1.1 copy.28
  (4 shorter events, 0.0 us)
Async XLA Ops:
  3.0 1.1 copy-start
  4.1 1.1 copy-start.1
  5.2 0.9 copy-start.2
  6.2 0.9 copy-start.3
  112.2 2.8 %copy-start.4 = (f32[1536,256]{1,0:T(8,128)S(1)}, f32[1536,256]{1,0:T(8,128)}, u32[]{:S(2)}) copy-start(f32[1536,256]{1,0:T(8,128)} %get-tuple-element.11) | copy-start | bytes 4718596

commit v2 on v1

--- a/solution.py
+++ b/solution.py
@@ -46,18 +46,25 @@
 
 
 def kernel(
-    sizes, tab, act, cot, w1, w2, mixed, gin, g1, g2,
-    ext, wb, band, v1, v2, vb, pre1, back, part, rs_out, rs_in, tot,
+    sizes, tab, act_in, cot_in, w1_in, w2_in, mixed, gin, g1, g2,
+    act, cot, w1, w2, ext, wb, band, v1, v2, vb, pre1, back, part, rs_out, rs_in, tot,
     s_right, r_right, s_left, r_left, ag_out, ag_in,
     x_send, x_recv, w_send, w_recv, f_send, f_recv, rs_send, rs_recv, c_send, c_recv,
-    ag_send, ag_recv,
+    ag_send, ag_recv, in_sem,
 ):
     nlat, nchan, nlon, chunks = sizes
-    rows, cols, width = act.shape
+    first_ticks, mid_ticks = chunks - 1, chunks
+    rows, cols, width = act_in.shape
     channels = nchan * width
     wide = cols + 2 * EDGE
     lat, chan, lon = lax.axis_index("lat"), lax.axis_index("chan"), lax.axis_index("lon")
     has_up, has_down = lat > 0, lat < nlat - 1
+    loads = [
+        pltpu.make_async_copy(src, dst, in_sem.at[n])
+        for n, (src, dst) in enumerate(((act_in, act), (w1_in, w1), (w2_in, w2), (cot_in, cot)))
+    ]
+    for load in loads:
+        load.start()
     mid = pl.ds(EDGE, cols)
 
     @pl.when(lat == 0)
@@ -175,7 +182,7 @@
             {"lat": lat - 1 if down else lat + 1, "chan": chan_at(-step)},
         ).wait_recv()
 
-    def finish_exchange(x):
+    def finish_middle(x):
         @pl.when(has_up)
         def _():
             for step in range(nchan):
@@ -190,8 +197,14 @@
             block_copy(x, step, chan_at(-step)).wait_recv()
         col_copy(x, True).start()
         col_copy(x, False).start()
+
+    def finish_columns(x):
         col_copy(x, True).wait_recv()
         col_copy(x, False).wait_recv()
+
+    def finish_exchange(x):
+        finish_middle(x)
+        finish_columns(x)
 
     def end_exchange(x):
         on_rows(x, lambda c: c.wait_send(), True)
@@ -265,113 +278,120 @@
                 g, pl.ds(pl.multiple_of(lon_at(step) * share, share), share)].astype(BF16)
             rs_copy(g, step).start()
 
-    def chain_copy(g, j, right):
+    def chain_copy(j, right):
         out, into = (s_right, r_right) if right else (s_left, r_left)
         side = 0 if right else 1
         return remote(
-            out.at[g, j], into.at[g, j], c_send.at[g, side, j], c_recv.at[g, side, j],
+            out.at[j], into.at[j], c_send.at[side, j], c_recv.at[side, j],
             {"lat": lat + 1 if right else lat - 1},
         )
 
-    def chain_wait(g, j, right):
+    def chain_wait(j, right):
         into = r_right if right else r_left
         side = 0 if right else 1
         remote(
-            into.at[g, j], into.at[g, j], c_send.at[g, side, j], c_recv.at[g, side, j],
+            into.at[j], into.at[j], c_send.at[side, j], c_recv.at[side, j],
             {"lat": lat - 1 if right else lat + 1},
         ).wait_recv()
 
-    def ag_copy(g, j, step):
-        return remote(
-            ag_out.at[g, j], ag_in.at[g, step - 1, j], ag_send.at[g, step - 1, j],
-            ag_recv.at[g, step - 1, j], {"lon": lon_at(step)},
-        )
-
-    def chain(g, out):
+    def ag_copy(j, step):
+        return remote(
+            ag_out.at[j], ag_in.at[step - 1, j], ag_send.at[step - 1, j],
+            ag_recv.at[step - 1, j], {"lon": lon_at(step)},
+        )
+
+    def prepare(g):
         for step in range(1, nlon):
             rs_copy(g, step).wait_recv()
         own = part[g, pl.ds(pl.multiple_of(lon * share, share), share)]
         for step in range(1, nlon):
             own = own + rs_in[g, step - 1].astype(F32)
-        tot[g] = own.reshape(chunks, piece, width)
-        rest = nlat - 1 - lat
-        late = jnp.maximum(lat, rest)
-
-        def tick(time, carry):
-            j_right = time - lat
-            j_left = time - rest
-            j_done = time - late
-
-            @pl.when((j_right >= 0) & (j_right < chunks) & (lat == 0))
+        tot[g * chunks:(g + 1) * chunks] = own.reshape(chunks, piece, width)
+
+    rest = nlat - 1 - lat
+    late = jnp.maximum(lat, rest)
+    both = 2 * chunks
+
+    def tick(time, carry):
+        j_right = time - lat
+        j_left = time - rest
+        j_done = time - late
+        do_right = (j_right >= 0) & (j_right < both)
+        do_left = (j_left >= 0) & (j_left < both)
+
+        @pl.when(do_right & (lat == 0))
+        def _():
+            s_right[j_right] = tot[j_right].astype(BF16)
+
+        @pl.when(do_right & (lat > 0))
+        def _():
+            chain_wait(j_right, True)
+            s_right[j_right] = (tot[j_right] + r_right[j_right].astype(F32)).astype(BF16)
+
+        @pl.when(do_right & has_down)
+        def _():
+            chain_copy(j_right, True).start()
+
+        @pl.when(do_left & (rest == 0))
+        def _():
+            s_left[j_left] = tot[j_left].astype(BF16)
+
+        @pl.when(do_left & (rest > 0))
+        def _():
+            chain_wait(j_left, False)
+            s_left[j_left] = (tot[j_left] + r_left[j_left].astype(F32)).astype(BF16)
+
+        @pl.when(do_left & has_up)
+        def _():
+            chain_copy(j_left, False).start()
+
+        @pl.when((j_done >= 0) & (j_done < both))
+        def _():
+            @pl.when(has_up)
             def _():
-                s_right[g, j_right] = tot[g, j_right].astype(BF16)
-
-            @pl.when((j_right >= 0) & (j_right < chunks) & (lat > 0))
-            def _():
-                chain_wait(g, j_right, True)
-                s_right[g, j_right] = (tot[g, j_right] + r_right[g, j_right].astype(F32)).astype(BF16)
-
-            @pl.when((j_right >= 0) & (j_right < chunks) & has_down)
-            def _():
-                chain_copy(g, j_right, True).start()
-
-            @pl.when((j_left >= 0) & (j_left < chunks) & (rest == 0))
-            def _():
-                s_left[g, j_left] = tot[g, j_left].astype(BF16)
-
-            @pl.when((j_left >= 0) & (j_left < chunks) & (rest > 0))
-            def _():
-                chain_wait(g, j_left, False)
-                s_left[g, j_left] = (tot[g, j_left] + r_left[g, j_left].astype(F32)).astype(BF16)
-
-            @pl.when((j_left >= 0) & (j_left < chunks) & has_up)
-            def _():
-                chain_copy(g, j_left, False).start()
-
-            @pl.when((j_done >= 0) & (j_done < chunks))
-            def _():
-                @pl.when(has_up)
-                def _():
-                    tot[g, j_done] = tot[g, j_done] + r_right[g, j_done].astype(F32)
-
-                @pl.when(has_down)
-                def _():
-                    tot[g, j_done] = tot[g, j_done] + r_left[g, j_done].astype(F32)
-
-                ag_out[g, j_done] = tot[g, j_done].astype(BF16)
-                for step in range(1, nlon):
-                    ag_copy(g, j_done, step).start()
-
-            return carry
-
-        lax.fori_loop(0, nlat - 1 + chunks, tick, 0)
-        out[pl.ds(pl.multiple_of(lon * share, share), share)] = tot[g].reshape(share, width)
-
-    def chain_end(g, out):
-        def settle(j, carry):
-            for step in range(1, nlon):
-                ag_copy(g, j, step).wait_recv()
-                ag_copy(g, j, step).wait_send()
+                tot[j_done] = tot[j_done] + r_right[j_done].astype(F32)
 
             @pl.when(has_down)
             def _():
-                chain_copy(g, j, True).wait_send()
+                tot[j_done] = tot[j_done] + r_left[j_done].astype(F32)
+
+            ag_out[j_done] = tot[j_done].astype(BF16)
+            for step in range(1, nlon):
+                ag_copy(j_done, step).start()
+
+        return carry
+
+    def settle():
+        def one(j, carry):
+            for step in range(1, nlon):
+                ag_copy(j, step).wait_recv()
+                ag_copy(j, step).wait_send()
+
+            @pl.when(has_down)
+            def _():
+                chain_copy(j, True).wait_send()
 
             @pl.when(has_up)
             def _():
-                chain_copy(g, j, False).wait_send()
+                chain_copy(j, False).wait_send()
 
             return carry
 
-        lax.fori_loop(0, chunks, settle, 0)
-        for step in range(1, nlon):
-            out[pl.ds(pl.multiple_of(lon_at(-step) * share, share), share)] = (
-                ag_in[g, step - 1].reshape(share, width).astype(F32)
-            )
-            rs_copy(g, step).wait_send()
-
+        lax.fori_loop(0, both, one, 0)
+        for g, out in ((0, g2), (1, g1)):
+            span = slice(g * chunks, (g + 1) * chunks)
+            out[pl.ds(pl.multiple_of(lon * share, share), share)] = ag_out[span].reshape(share, width)
+            for step in range(1, nlon):
+                out[pl.ds(pl.multiple_of(lon_at(-step) * share, share), share)] = (
+                    ag_in[step - 1, span].reshape(share, width)
+                )
+                rs_copy(g, step).wait_send()
+
+    loads[0].wait()
     put(0, act[...])
     start_exchange(0)
+    for load in loads[1:]:
+        load.wait()
     for which in (1, 0):
         for step in range(1, nchan):
             weight_copy(which, step, chan_at(step), chan).start()
@@ -406,6 +426,8 @@
         for step in range(1, nchan):
             for hop in range(1, nlon):
                 forward_copy(which, step, hop, lon_at(-hop)).wait_recv()
+    prepare(0)
+    lax.fori_loop(0, first_ticks, tick, 0)
     finish_exchange(2)
     apply_filter(1, 2, vb)
     back_hidden = (cot[...].reshape(rows * cols, width).astype(F32) + mix_back(1)).astype(BF16)
@@ -414,13 +436,15 @@
     put(3, dpre1)
     start_exchange(3)
     weight_gradient(1, v1, dpre1)
-    chain(0, g2)
-    finish_exchange(3)
+    lax.fori_loop(first_ticks, chunks, tick, 0)
+    prepare(1)
+    lax.fori_loop(chunks, chunks + mid_ticks, tick, 0)
+    finish_middle(3)
+    lax.fori_loop(chunks + mid_ticks, nlat - 1 + both, tick, 0)
+    finish_columns(3)
     apply_filter(1, 3, vb)
     gin[...] = (back[...].astype(F32) + mix_back(0)).reshape(rows, cols, width)
-    chain(1, g1)
-    chain_end(0, g2)
-    chain_end(1, g1)
+    settle()
     for x in range(4):
         end_exchange(x)
     for which in (1, 0):
@@ -450,12 +474,16 @@
         out_shape=(
             jax.ShapeDtypeStruct((rows, cols, width), BF16),
             jax.ShapeDtypeStruct((rows, cols, width), F32),
-            jax.ShapeDtypeStruct((full_rows, width), F32),
-            jax.ShapeDtypeStruct((full_rows, width), F32),
+            jax.ShapeDtypeStruct((full_rows, width), BF16),
+            jax.ShapeDtypeStruct((full_rows, width), BF16),
         ),
-        in_specs=[pl.BlockSpec(memory_space=pltpu.SMEM)] + [vmem] * 4,
+        in_specs=[pl.BlockSpec(memory_space=pltpu.SMEM)] + [pl.BlockSpec(memory_space=pltpu.HBM)] * 4,
         out_specs=(vmem,) * 4,
         scratch_shapes=[
+            pltpu.VMEM((rows, cols, width), BF16),
+            pltpu.VMEM((rows, cols, width), BF16),
+            pltpu.VMEM((KB, channels, width), BF16),
+            pltpu.VMEM((KB, channels, width), BF16),
             pltpu.VMEM((4, nchan, rows + 2, wide, width), BF16),
             pltpu.VMEM((2, KB, width, channels), BF16),
             pltpu.VMEM((2, rows, KB * cols, 3 * wide), BF16),
@@ -467,13 +495,13 @@
             pltpu.VMEM((2, full_rows, width), F32),
             pltpu.VMEM((2, nlon - 1, share, width), BF16),
             pltpu.VMEM((2, nlon - 1, share, width), BF16),
-            pltpu.VMEM((2, chunks, piece, width), F32),
-            pltpu.VMEM((2, chunks, piece, width), BF16),
-            pltpu.VMEM((2, chunks, piece, width), BF16),
-            pltpu.VMEM((2, chunks, piece, width), BF16),
-            pltpu.VMEM((2, chunks, piece, width), BF16),
-            pltpu.VMEM((2, chunks, piece, width), BF16),
-            pltpu.VMEM((2, nlon - 1, chunks, piece, width), BF16),
+            pltpu.VMEM((2 * chunks, piece, width), F32),
+            pltpu.VMEM((2 * chunks, piece, width), BF16),
+            pltpu.VMEM((2 * chunks, piece, width), BF16),
+            pltpu.VMEM((2 * chunks, piece, width), BF16),
+            pltpu.VMEM((2 * chunks, piece, width), BF16),
+            pltpu.VMEM((2 * chunks, piece, width), BF16),
+            pltpu.VMEM((nlon - 1, 2 * chunks, piece, width), BF16),
             dma((4, slots)),
             dma((4, slots)),
             dma((2, nchan)),
@@ -482,21 +510,22 @@
             dma((2, nchan, nlon)),
             dma((2, nlon - 1)),
             dma((2, nlon - 1)),
-            dma((2, 2, chunks)),
-            dma((2, 2, chunks)),
-            dma((2, nlon - 1, chunks)),
-            dma((2, nlon - 1, chunks)),
+            dma((2, 2 * chunks)),
+            dma((2, 2 * chunks)),
+            dma((nlon - 1, 2 * chunks)),
+            dma((nlon - 1, 2 * chunks)),
+            dma((4,)),
         ],
         compiler_params=pltpu.CompilerParams(
             collective_id=0, has_side_effects=True, vmem_limit_bytes=50 * 1024 * 1024
         ),
     )(near, activations, cotangent, w_first, w_second)
     shape = (KB, channels, width)
-    return mixed, gin, g1.reshape(shape), g2.reshape(shape)
+    return mixed, gin, g1.astype(F32).reshape(shape), g2.astype(F32).reshape(shape)
 
 
 def solution(mesh):
-    sizes = (mesh.shape["lat"], mesh.shape["chan"], mesh.shape["lon"], 8)
+    sizes = (mesh.shape["lat"], mesh.shape["chan"], mesh.shape["lon"], 3)
     return jax.shard_map(
         functools.partial(body, sizes),
         mesh=mesh,

time: 116 us -> 80.9 us (0.70)
  Pallas kernels: 104 us -> 70.6 us
  local copies, waits for them, and re-layouts: 10.3 us -> 5.22 us
  other arithmetic: 1.52 us -> 4.07 us
    pallas_call x1, Pallas kernels: 104 us -> 70.6 us  [body(): pl.pallas_call(functools.partial(kernel, sizes), out_shape=(jax.ShapeDtyp...]
    unnamed x15 -> x9, local copies, waits for them, and re-layouts: 10.2 us -> 5.11 us
    reshape x0 -> x2, other arithmetic: none -> 2.55 us  [the longest x1 1.28 us: body(): g1.astype(F32).reshape(shape)]
where the time goes in v2:
time: 80.9 us; the launch traced here: 80.5 us
  Pallas kernels  70.6 us (87%)
  local copies, waits for them, and re-layouts  5.22 us (6%)
  other arithmetic  4.07 us (5%)
    pallas_call x1, Pallas kernels, body(): pl.pallas_call(functools.partial(kernel, sizes), out_shape=(jax.ShapeDtyp...  70.6 us
    unnamed x9, local copies, waits for them, and re-layouts  5.11 us

profile of v2, /device:TPU:0, one launch (start us, length us, event | category | flops | bytes accessed | tf_op | source)
XLA Modules:
  0.0 80.5 jit_solution(10120751175464431572)
XLA Ops:
  0.6 0.7 iota_compare_fusion.1
  1.3 0.8 iota_compare_fusion
  2.1 0.7 copy.19
  2.8 0.1 select_reduce_fusion
  2.9 0.1 copy.20
  3.0 0.0 copy-start
  3.0 1.1 %copy-done = bf16[3,512,256]{2,1,0:T(8,128)(2,1)S(1)} copy-done((bf16[3,512,256]{2,1,0:T(8,128)(2,1)S(1)}, bf16[3,512,256]{2,1,0:T(8,128)(2,1)}, u32[]{:S(2)}) %copy-start) | copy-done | bytes 786456
  4.1 0.0 copy-start.1
  4.1 0.9 %copy-done.1 = bf16[4,96,256]{2,1,0:T(8,128)(2,1)S(1)} copy-done((bf16[4,96,256]{2,1,0:T(8,128)(2,1)S(1)}, bf16[4,96,256]{2,1,0:T(8,128)(2,1)}, u32[]{:S(2)}) %copy-start.1) | copy-done | bytes 196632
  5.0 0.0 copy-start.2
  5.0 0.9 %copy-done.2 = bf16[4,96,256]{2,1,0:T(8,128)(2,1)S(1)} copy-done((bf16[4,96,256]{2,1,0:T(8,128)(2,1)S(1)}, bf16[4,96,256]{2,1,0:T(8,128)(2,1)}, u32[]{:S(2)}) %copy-start.2) | copy-done | bytes 196632
  6.0 70.6 %shard_map.111 = (bf16[4,96,256]{2,1,0:T(8,128)(2,1)S(1)}, f32[4,96,256]{2,1,0:T(8,128)S(1)}, bf16[1536,256]{1,0:T(8,128)(2,1)S(1)}, bf16[1536,256]{1,0:T(8,128)(2,1)S(1)}) custom-call(f32[6,27]{1,0:T(8,128)S(1)} %pad_dynamic-slice_fusion.tab, bf16[4,96,256]{2,1,0:T(8,128)(2,1)S(1)} %copy-done.1, bf16[4,96,256]{2,1,0:T(8,128)(2,1)S(1)} %copy-done.2, ...), custom_call_target="tpu_custom_call" | custom-call | tf_op jit(solution)/shard_map/pallas_call | solution.py:472
  76.6 1.3 %convert.2 = f32[3,512,256]{2,1,0:T(8,128)} convert(bf16[3,512,256]{2,1,0:T(8,128)(2,1)S(1)} %bitcast.7) | non-fusion elementwise | flops 393216 | bytes 2359296 | tf_op jit(solution)/shard_map/reshape | solution.py:524
  77.9 1.3 %convert.3 = f32[3,512,256]{2,1,0:T(8,128)} convert(bf16[3,512,256]{2,1,0:T(8,128)(2,1)S(1)} %bitcast.6) | non-fusion elementwise | flops 393216 | bytes 2359296 | tf_op jit(solution)/shard_map/reshape | solution.py:524
  79.1 0.7 copy.23
  79.8 0.7 copy.24
  (4 shorter events, 0.0 us)
Async XLA Ops:
  3.0 1.1 %copy-start = (bf16[3,512,256]{2,1,0:T(8,128)(2,1)S(1)}, bf16[3,512,256]{2,1,0:T(8,128)(2,1)}, u32[]{:S(2)}) copy-start(bf16[3,512,256]{2,1,0:T(8,128)(2,1)} %w1_in.1) | copy-start | bytes 2359300
  4.1 0.9 %copy-start.1 = (bf16[4,96,256]{2,1,0:T(8,128)(2,1)S(1)}, bf16[4,96,256]{2,1,0:T(8,128)(2,1)}, u32[]{:S(2)}) copy-start(bf16[4,96,256]{2,1,0:T(8,128)(2,1)} %act_in.1) | copy-start | bytes 589828
  5.0 0.9 %copy-start.2 = (bf16[4,96,256]{2,1,0:T(8,128)(2,1)S(1)}, bf16[4,96,256]{2,1,0:T(8,128)(2,1)}, u32[]{:S(2)}) copy-start(bf16[4,96,256]{2,1,0:T(8,128)(2,1)} %cot_in.1) | copy-start | bytes 589828

commit v3 on v2

--- a/solution.py
+++ b/solution.py
@@ -53,7 +53,7 @@
     ag_send, ag_recv, in_sem,
 ):
     nlat, nchan, nlon, chunks = sizes
-    first_ticks, mid_ticks = chunks - 1, chunks
+    first_ticks, mid_ticks = chunks, chunks
     rows, cols, width = act_in.shape
     channels = nchan * width
     wide = cols + 2 * EDGE
@@ -234,6 +234,12 @@
             {"lon": lon_at(hop)},
         )
 
+    def pass_on(which):
+        for step in range(1, nchan):
+            weight_copy(which, step, chan, chan_at(-step)).wait_recv()
+            for hop in range(1, nlon):
+                forward_copy(which, step, hop, lon).start()
+
     def apply_filter(which, x, out):
         for i in range(rows):
             for slot in range(nchan):
@@ -392,27 +398,26 @@
     start_exchange(0)
     for load in loads[1:]:
         load.wait()
-    for which in (1, 0):
-        for step in range(1, nchan):
-            weight_copy(which, step, chan_at(step), chan).start()
     build_band(0)
     build_band(1)
     for which in (1, 0):
         wb[which, :, :, pl.ds(pl.multiple_of(chan * width, width), width)] = weights[which][
             :, pl.ds(pl.multiple_of(chan * width, width), width)]
-    finish_exchange(0)
+    finish_middle(0)
+    for step in range(1, nchan):
+        weight_copy(1, step, chan_at(step), chan).start()
+    finish_columns(0)
     apply_filter(0, 0, v1)
     first = jnp.dot(v1[...], w1[...].reshape(full_rows, width), preferred_element_type=F32)
     pre1[...] = first
     hidden = (act[...].reshape(rows * cols, width).astype(F32) + gelu(first)).astype(BF16)
     put(1, hidden)
     start_exchange(1)
-    for which in (1, 0):
-        for step in range(1, nchan):
-            weight_copy(which, step, chan, chan_at(-step)).wait_recv()
-            for hop in range(1, nlon):
-                forward_copy(which, step, hop, lon).start()
-    finish_exchange(1)
+    pass_on(1)
+    finish_middle(1)
+    for step in range(1, nchan):
+        weight_copy(0, step, chan_at(step), chan).start()
+    finish_columns(1)
     apply_filter(0, 1, v2)
     second = jnp.dot(v2[...], w2[...].reshape(full_rows, width), preferred_element_type=F32)
     upstream = cot[...].reshape(rows * cols, width).astype(F32)
@@ -422,6 +427,7 @@
     held = ext[1, chan, 1:rows + 1, mid].reshape(rows * cols, width).astype(F32)
     mixed[...] = (held + gelu(second)).astype(BF16).reshape(rows, cols, width)
     weight_gradient(0, v2, dpre2)
+    pass_on(0)
     for which in (1, 0):
         for step in range(1, nchan):
             for hop in range(1, nlon):
@@ -525,7 +531,7 @@
 
 
 def solution(mesh):
-    sizes = (mesh.shape["lat"], mesh.shape["chan"], mesh.shape["lon"], 3)
+    sizes = (mesh.shape["lat"], mesh.shape["chan"], mesh.shape["lon"], 2)
     return jax.shard_map(
         functools.partial(body, sizes),
         mesh=mesh,

time: 80.9 us -> 76.2 us (0.942)
  Pallas kernels: 70.6 us -> 65.9 us
    pallas_call x1, Pallas kernels: 70.6 us -> 65.9 us  [body(): pl.pallas_call(functools.partial(kernel, sizes), out_shape=(jax.ShapeDtyp...]
where the time goes in v3:
time: 76.2 us; the launch traced here: 75.8 us
  Pallas kernels  65.9 us (86%)
  local copies, waits for them, and re-layouts  5.22 us (7%)
  other arithmetic  4.07 us (5%)
    pallas_call x1, Pallas kernels, body(): pl.pallas_call(functools.partial(kernel, sizes), out_shape=(jax.ShapeDtyp...  65.9 us
    unnamed x9, local copies, waits for them, and re-layouts  5.11 us

profile of v3, /device:TPU:0, one launch (start us, length us, event | category | flops | bytes accessed | tf_op | source)
XLA Modules:
  0.0 75.8 jit_solution(3587923758543617917)
XLA Ops:
  0.6 0.7 iota_compare_fusion.1
  1.3 0.8 %iota_compare_fusion = (pred[16,6,3]{0,1,2:T(8,128)(4,1)S(1)}, pred[16,6,3]{0,1,2:T(8,128)(4,1)S(1)}) fusion(s32[16,6]{0,1:T(8,128)} %param.13, pred[16,6]{0,1:T(8,128)(4,1)S(1)} %iota_compare_fusion.1, s32[3]{0:T(128)S(1)} %iota_add_fusion, s32[16,6]{0,1:T(8,128)} %param.12), kind=kLoop, calls=%fused_computation.3 | loop fusion | flops 864 | bytes 1452 | tf_op jit(solution)/shard_map/eq | solution.py:28
  2.1 0.7 copy.19
  2.8 0.1 select_reduce_fusion
  2.9 0.1 copy.20
  3.0 0.0 copy-start
  3.0 1.1 %copy-done = bf16[3,512,256]{2,1,0:T(8,128)(2,1)S(1)} copy-done((bf16[3,512,256]{2,1,0:T(8,128)(2,1)S(1)}, bf16[3,512,256]{2,1,0:T(8,128)(2,1)}, u32[]{:S(2)}) %copy-start) | copy-done | bytes 786456
  4.1 0.0 copy-start.1
  4.1 0.9 %copy-done.1 = bf16[4,96,256]{2,1,0:T(8,128)(2,1)S(1)} copy-done((bf16[4,96,256]{2,1,0:T(8,128)(2,1)S(1)}, bf16[4,96,256]{2,1,0:T(8,128)(2,1)}, u32[]{:S(2)}) %copy-start.1) | copy-done | bytes 196632
  5.0 0.0 copy-start.2
  5.0 0.9 %copy-done.2 = bf16[4,96,256]{2,1,0:T(8,128)(2,1)S(1)} copy-done((bf16[4,96,256]{2,1,0:T(8,128)(2,1)S(1)}, bf16[4,96,256]{2,1,0:T(8,128)(2,1)}, u32[]{:S(2)}) %copy-start.2) | copy-done | bytes 196632
  6.0 65.9 %shard_map.111 = (bf16[4,96,256]{2,1,0:T(8,128)(2,1)S(1)}, f32[4,96,256]{2,1,0:T(8,128)S(1)}, bf16[1536,256]{1,0:T(8,128)(2,1)S(1)}, bf16[1536,256]{1,0:T(8,128)(2,1)S(1)}) custom-call(f32[6,27]{1,0:T(8,128)S(1)} %pad_dynamic-slice_fusion.tab, bf16[4,96,256]{2,1,0:T(8,128)(2,1)S(1)} %copy-done.1, bf16[4,96,256]{2,1,0:T(8,128)(2,1)S(1)} %copy-done.2, ...), custom_call_target="tpu_custom_call" | custom-call | tf_op jit(solution)/shard_map/pallas_call | solution.py:478
  71.9 1.3 %convert.2 = f32[3,512,256]{2,1,0:T(8,128)} convert(bf16[3,512,256]{2,1,0:T(8,128)(2,1)S(1)} %bitcast.7) | non-fusion elementwise | flops 393216 | bytes 2359296 | tf_op jit(solution)/shard_map/reshape | solution.py:530
  73.1 1.3 %convert.3 = f32[3,512,256]{2,1,0:T(8,128)} convert(bf16[3,512,256]{2,1,0:T(8,128)(2,1)S(1)} %bitcast.6) | non-fusion elementwise | flops 393216 | bytes 2359296 | tf_op jit(solution)/shard_map/reshape | solution.py:530
  74.4 0.7 copy.23
  75.1 0.7 copy.24
  (4 shorter events, 0.0 us)
Async XLA Ops:
  3.0 1.1 %copy-start = (bf16[3,512,256]{2,1,0:T(8,128)(2,1)S(1)}, bf16[3,512,256]{2,1,0:T(8,128)(2,1)}, u32[]{:S(2)}) copy-start(bf16[3,512,256]{2,1,0:T(8,128)(2,1)} %w1_in.1) | copy-start | bytes 2359300
  4.1 0.9 %copy-start.1 = (bf16[4,96,256]{2,1,0:T(8,128)(2,1)S(1)}, bf16[4,96,256]{2,1,0:T(8,128)(2,1)}, u32[]{:S(2)}) copy-start(bf16[4,96,256]{2,1,0:T(8,128)(2,1)} %act_in.1) | copy-start | bytes 589828
  5.0 0.9 %copy-start.2 = (bf16[4,96,256]{2,1,0:T(8,128)(2,1)S(1)}, bf16[4,96,256]{2,1,0:T(8,128)(2,1)}, u32[]{:S(2)}) copy-start(bf16[4,96,256]{2,1,0:T(8,128)(2,1)} %cot_in.1) | copy-start | bytes 589828
